TPU v7x, 32 devices: a whole 2x2x4 slice. The times are simulated.
32 devices in a mesh: row: 8 (over z, y), col: 4 (over x, core).
Axes of the slice: x: 2, y: 2, z: 4, core: 2. Of those that a mesh axis runs over, the one named last changes fastest.
Arguments:
- sources: float32 [16384, 256], P(('row', 'col')), may hold values from -6 to 6
- level_factors: float32 [8, 128, 2, 128, 128], P(None, ('row', 'col')), may hold values from -0.375 to 0.375
Outputs:
- fields: float32 [4096, 256], P(('row', 'col'))
All inputs are finite; a program needn't handle non-finite values.
Results may differ from a plain program's by a relative error of at most 0.00012.
Values sent between devices are 32-bit elements; how exact they have to be, the bound alone decides.
A program may use at most 64 MiB of HBM per device.

v0:
```python
import jax
import jax.numpy as jnp
from jax import lax
from jax.sharding import PartitionSpec as P

ROW_LEVELS = 5
COL_LEVELS = 3


def swapped(value, axis, bit):
    mask = 2**bit
    pairs = [(source, source ^ mask) for source in range(lax.axis_size(axis))]
    return lax.ppermute(value, axis, pairs)


def mix_level(factors, state, partner):
    own_term = jnp.einsum("bij,bjr->bir", factors[:, 0], state, precision=lax.Precision.HIGHEST)
    return own_term + jnp.einsum(
        "bij,bjr->bir", factors[:, 1], partner, precision=lax.Precision.HIGHEST
    )


def shards(sources, level_factors):
    blocks_here = level_factors.shape[1]
    width = level_factors.shape[3]
    columns = sources.shape[1]
    state = sources.reshape(blocks_here, width, columns)
    log_row = lax.axis_size("row").bit_length() - 1
    log_col = lax.axis_size("col").bit_length() - 1
    last = ROW_LEVELS + COL_LEVELS - 1
    for level in range(ROW_LEVELS):
        partner = swapped(state, "row", level % log_row)
        state = mix_level(level_factors[level], state, partner)
    for level in range(ROW_LEVELS, last + 1):
        partner = swapped(state, "col", (level - ROW_LEVELS) % log_col)
        state = mix_level(level_factors[level], state, partner)
    total = state.reshape(blocks_here * width, columns)
    return lax.psum_scatter(total, "col", scatter_dimension=0, tiled=True)


def solution(mesh):
    return jax.shard_map(
        shards,
        mesh=mesh,
        in_specs=(P(("row", "col"), None), P(None, ("row", "col"), None, None, None)),
        out_specs=P(("row", "col"), None),
        check_vma=False,
    )
```

profile of v0, /device:TPU:0, one launch (start us, length us, event | category | flops | bytes accessed | tf_op | source)
XLA Modules:
  0.0 139.7 jit_solution(7126712620110440850)
XLA Ops:
  6.5 0.0 reduce-scatter.2.cloned.1.call-start
  6.5 0.0 copy-start
  6.5 3.0 %collective-permute-start = (f32[4,128,256]{2,1,0:T(8,128)}, f32[4,128,256]{2,1,0:T(8,128)S(1)}, u32[]{:S(2)}, u32[]{:S(2)}) collective-permute-start(f32[4,128,256]{2,1,0:T(8,128)} %bitcast.121), channel_id=1, source_target_pairs={{0,4},{4,0},{8,12},{12,8},{16,20},{20,16},{24,28},{28,24},{1,5},{5... | collective-permute-start | bytes 1572872 | tf_op jit(solution)/shard_map/ppermute | solution.py:13
  9.5 2.4 %fusion.8 = (f32[1,4,2,128,128]{4,3,2,1,0:T(8,128)S(1)}, f32[1,4,2,128,128]{4,3,2,1,0:T(8,128)S(1)}, f32[1,4,2,128,128]{4,3,2,1,0:T(8,128)S(1)}, f32[1,4,2,128,1...) fusion(f32[8,4,2,128,128]{4,3,2,1,0:T(8,128)} %param.3), kind=kLoop, calls=%fused_computation.40 | loop fusion | bytes 8388608 | tf_op jit(solution)/shard_map/slice | solution.py:36
  12.0 0.0 copy-done
  12.0 0.6 fusion.7
  12.6 9.1 %collective-permute-done = f32[4,128,256]{2,1,0:T(8,128)S(1)} collective-permute-done((f32[4,128,256]{2,1,0:T(8,128)}, f32[4,128,256]{2,1,0:T(8,128)S(1)}, u32[]{:S(2)}, u32[]{:S(2)}) %collective-permute-start) | collective-permute-done | bytes 524320 | tf_op jit(solution)/shard_map/ppermute | solution.py:13
  21.7 0.6 convolution_add_fusion.7
  22.3 1.8 %collective-permute-start.1 = (f32[4,128,256]{2,1,0:T(8,128)S(1)}, f32[4,128,256]{2,1,0:T(8,128)S(1)}, u32[]{:S(2)}, u32[]{:S(2)}) collective-permute-start(f32[4,128,256]{2,1,0:T(8,128)S(1)} %convolution_add_fusion.7), channel_id=1, source_target_pairs={{0,8},{4,12},{8,0},{12,4},{16,24},{20,28},{24,16},{28,20},{1,9},{5... | collective-permute-start | bytes 1572872 | tf_op jit(solution)/shard_map/ppermute | solution.py:13
  24.1 1.1 fusion.6
  25.2 10.3 %collective-permute-done.1 = f32[4,128,256]{2,1,0:T(8,128)S(1)} collective-permute-done((f32[4,128,256]{2,1,0:T(8,128)S(1)}, f32[4,128,256]{2,1,0:T(8,128)S(1)}, u32[]{:S(2)}, u32[]{:S(2)}) %collective-permute-start.1) | collective-permute-done | bytes 524320 | tf_op jit(solution)/shard_map/ppermute | solution.py:13
  35.5 1.1 convolution_add_fusion.6
  36.5 2.5 %collective-permute-start.2 = (f32[4,128,256]{1,2,0:T(8,128)S(1)}, f32[4,128,256]{1,2,0:T(8,128)S(1)}, u32[]{:S(2)}, u32[]{:S(2)}) collective-permute-start(f32[4,128,256]{1,2,0:T(8,128)S(1)} %bitcast.100), channel_id=1, source_target_pairs={{0,16},{4,20},{8,24},{12,28},{16,0},{20,4},{24,8},{28,12},{1,17},{... | collective-permute-start | bytes 1572872 | tf_op jit(solution)/shard_map/ppermute | solution.py:13
  39.1 0.6 fusion.5
  39.7 21.2 %collective-permute-done.2 = f32[4,128,256]{1,2,0:T(8,128)S(1)} collective-permute-done((f32[4,128,256]{1,2,0:T(8,128)S(1)}, f32[4,128,256]{1,2,0:T(8,128)S(1)}, u32[]{:S(2)}, u32[]{:S(2)}) %collective-permute-start.2) | collective-permute-done | bytes 524320 | tf_op jit(solution)/shard_map/ppermute | solution.py:13
  60.9 0.6 convolution_add_fusion.5
  61.5 1.1 collective-permute-start.3
  62.7 0.6 fusion.4
  63.3 11.5 %collective-permute-done.3 = f32[4,128,256]{1,2,0:T(8,128)S(1)} collective-permute-done((f32[4,128,256]{1,2,0:T(8,128)S(1)}, f32[4,128,256]{1,2,0:T(8,128)S(1)}, u32[]{:S(2)}, u32[]{:S(2)}) %collective-permute-start.3) | collective-permute-done | bytes 524320 | tf_op jit(solution)/shard_map/ppermute | solution.py:13
  74.9 0.6 convolution_add_fusion.4
  75.5 0.9 collective-permute-start.4
  76.4 0.6 fusion.3
  77.0 10.9 %collective-permute-done.4 = f32[4,128,256]{1,2,0:T(8,128)S(1)} collective-permute-done((f32[4,128,256]{1,2,0:T(8,128)S(1)}, f32[4,128,256]{1,2,0:T(8,128)S(1)}, u32[]{:S(2)}, u32[]{:S(2)}) %collective-permute-start.4) | collective-permute-done | bytes 524320 | tf_op jit(solution)/shard_map/ppermute | solution.py:13
  87.9 0.6 convolution_add_fusion.3
  88.5 0.1 collective-permute-start.5
  88.6 0.6 fusion.2
  89.2 1.2 collective-permute-done.5
  90.5 0.6 convolution_add_fusion.2
  91.1 1.3 collective-permute-start.6
  92.4 0.6 fusion.1
  93.0 12.1 %collective-permute-done.6 = f32[4,128,256]{1,2,0:T(8,128)S(1)} collective-permute-done((f32[4,128,256]{1,2,0:T(8,128)S(1)}, f32[4,128,256]{1,2,0:T(8,128)S(1)}, u32[]{:S(2)}, u32[]{:S(2)}) %collective-permute-start.6) | collective-permute-done | bytes 524320 | tf_op jit(solution)/shard_map/ppermute | solution.py:13
  105.1 0.6 convolution_add_fusion.1
  105.8 0.1 collective-permute-start.7
  105.9 0.6 fusion
  106.5 1.2 collective-permute-done.7
  107.7 1.4 %convolution_add_fusion = f32[4,256,128]{1,2,0:T(8,128)} fusion(f32[4,256,128]{1,2,0:T(8,128)S(1)} %fusion, f32[4,128,256]{1,2,0:T(8,128)S(1)} %collective-permute-done.7, f32[4,2,128,128]{3,2,0,1:T(8,128)S(1)} %bitcast.118), kind=kOutput, calls=%fused_computation | convolution fusion | flops 201457664 | bytes 1835008 | tf_op jit(solution)/shard_map/bij,bjr->bir/dot_general | solution.py:18
  109.1 0.0 reduce-scatter.2.cloned.1.call-update
  109.2 23.7 %reduce-scatter.2.cloned.1.call-done = f32[128,256]{1,0:T(8,128)} async-done(((f32[512,256]{1,0:T(8,128)}), f32[128,256]{1,0:T(8,128)}) %reduce-scatter.2.cloned.1.call-update) | async-done | bytes 131088 | tf_op jit(solution)/shard_map/reduce_scatter | solution.py:38
  (8 shorter events, 0.3 us)
Async XLA Ops:
  6.5 126.4 %reduce-scatter.2.cloned.1.call-start = ((), (), s32[]{:S(2)}) async-start(), calls=%async_computation.1 | async-start | bytes 655360 | tf_op jit(solution)/shard_map/reduce_scatter | solution.py:38
  6.5 5.4 %copy-start = (f32[512,256]{1,0:T(8,128)S(1)}, f32[512,256]{1,0:T(8,128)}, u32[]{:S(2)}) copy-start(f32[512,256]{1,0:T(8,128)} %param.2) | copy-start | bytes 1572868
  6.5 15.2 %collective-permute-start = (f32[4,128,256]{2,1,0:T(8,128)}, f32[4,128,256]{2,1,0:T(8,128)S(1)}, u32[]{:S(2)}, u32[]{:S(2)}) collective-permute-start(f32[4,128,256]{2,1,0:T(8,128)} %bitcast.121), channel_id=1, source_target_pairs={{0,4},{4,0},{8,12},{12,8},{16,20},{20,16},{24,28},{28,24},{1,5},{5... | collective-permute-start | bytes 1572872 | tf_op jit(solution)/shard_map/ppermute | solution.py:13
  22.3 13.2 %collective-permute-start.1 = (f32[4,128,256]{2,1,0:T(8,128)S(1)}, f32[4,128,256]{2,1,0:T(8,128)S(1)}, u32[]{:S(2)}, u32[]{:S(2)}) collective-permute-start(f32[4,128,256]{2,1,0:T(8,128)S(1)} %convolution_add_fusion.7), channel_id=1, source_target_pairs={{0,8},{4,12},{8,0},{12,4},{16,24},{20,28},{24,16},{28,20},{1,9},{5... | collective-permute-start | bytes 1572872 | tf_op jit(solution)/shard_map/ppermute | solution.py:13
  36.5 24.4 %collective-permute-start.2 = (f32[4,128,256]{1,2,0:T(8,128)S(1)}, f32[4,128,256]{1,2,0:T(8,128)S(1)}, u32[]{:S(2)}, u32[]{:S(2)}) collective-permute-start(f32[4,128,256]{1,2,0:T(8,128)S(1)} %bitcast.100), channel_id=1, source_target_pairs={{0,16},{4,20},{8,24},{12,28},{16,0},{20,4},{24,8},{28,12},{1,17},{... | collective-permute-start | bytes 1572872 | tf_op jit(solution)/shard_map/ppermute | solution.py:13
  61.5 13.3 %collective-permute-start.3 = (f32[4,128,256]{1,2,0:T(8,128)S(1)}, f32[4,128,256]{1,2,0:T(8,128)S(1)}, u32[]{:S(2)}, u32[]{:S(2)}) collective-permute-start(f32[4,128,256]{1,2,0:T(8,128)S(1)} %bitcast.101), channel_id=1, source_target_pairs={{0,4},{4,0},{8,12},{12,8},{16,20},{20,16},{24,28},{28,24},{1,5},{5... | collective-permute-start | bytes 1572872 | tf_op jit(solution)/shard_map/ppermute | solution.py:13
  75.5 12.4 %collective-permute-start.4 = (f32[4,128,256]{1,2,0:T(8,128)S(1)}, f32[4,128,256]{1,2,0:T(8,128)S(1)}, u32[]{:S(2)}, u32[]{:S(2)}) collective-permute-start(f32[4,128,256]{1,2,0:T(8,128)S(1)} %bitcast.102), channel_id=1, source_target_pairs={{0,8},{4,12},{8,0},{12,4},{16,24},{20,28},{24,16},{28,20},{1,9},{5... | collective-permute-start | bytes 1572872 | tf_op jit(solution)/shard_map/ppermute | solution.py:13
  88.5 2.0 %collective-permute-start.5 = (f32[4,128,256]{1,2,0:T(8,128)S(1)}, f32[4,128,256]{1,2,0:T(8,128)S(1)}, u32[]{:S(2)}, u32[]{:S(2)}) collective-permute-start(f32[4,128,256]{1,2,0:T(8,128)S(1)} %bitcast.103), channel_id=1, source_target_pairs={{0,1},{1,0},{2,3},{3,2},{4,5},{5,4},{6,7},{7,6},{8,9},{9,8},{10,11... | collective-permute-start | bytes 1572872 | tf_op jit(solution)/shard_map/ppermute | solution.py:13
  91.1 14.0 %collective-permute-start.6 = (f32[4,128,256]{1,2,0:T(8,128)S(1)}, f32[4,128,256]{1,2,0:T(8,128)S(1)}, u32[]{:S(2)}, u32[]{:S(2)}) collective-permute-start(f32[4,128,256]{1,2,0:T(8,128)S(1)} %bitcast.104), channel_id=1, source_target_pairs={{0,2},{1,3},{2,0},{3,1},{4,6},{5,7},{6,4},{7,5},{8,10},{9,11},{10,... | collective-permute-start | bytes 1572872 | tf_op jit(solution)/shard_map/ppermute | solution.py:13
  105.8 2.0 %collective-permute-start.7 = (f32[4,128,256]{1,2,0:T(8,128)S(1)}, f32[4,128,256]{1,2,0:T(8,128)S(1)}, u32[]{:S(2)}, u32[]{:S(2)}) collective-permute-start(f32[4,128,256]{1,2,0:T(8,128)S(1)} %bitcast.98), channel_id=1, source_target_pairs={{0,1},{1,0},{2,3},{3,2},{4,5},{5,4},{6,7},{7,6},{8,9},{9,8},{10,11... | collective-permute-start | bytes 1572872 | tf_op jit(solution)/shard_map/ppermute | solution.py:13
Sparse Core Ops, SparseCore 0:
  109.3 23.5 reduce-scatter.1
where the time goes:
time: 140 us
  waiting for transfers between devices  101 us (72%)
  between operations  13.6 us (10%)
  matrix products  11.5 us (8%)
  starting transfers between devices  10.6 us (8%)
  local copies, waits for them, and re-layouts  2.7 us (2%)
    ppermute x8, waiting for transfers between devices, swapped(): return lax.ppermute(value, axis, pairs)  77.6 us
    reduce_scatter x1, waiting for transfers between devices, shards(): return lax.psum_scatter(total, 'col', scatter_dimension=0, tiled=True)  23.7 us
    ppermute x8, starting transfers between devices, swapped(): return lax.ppermute(value, axis, pairs)  10.6 us
    dot_general x8, matrix products, mix_level(): jnp.einsum('bij,bjr->bir', factors[:, 1], partner, precision=lax.Precisio...  6.13 us
    dot_general x8, matrix products, mix_level(): jnp.einsum('bij,bjr->bir', factors[:, 0], state, precision=lax.Precision....  5.33 us
  transfers between devices with their start and end apart: 9, of which 9 were waited for; matrix products, arithmetic and copies ran while one was open for 6% of the time, Pallas kernels for 0%

commit v1 on v0

v1 whole, which is shorter than its diff:
```python
import functools

import jax
import jax.numpy as jnp
from jax import lax
from jax.experimental import pallas as pl
from jax.experimental.pallas import tpu as pltpu
from jax.sharding import PartitionSpec as P

ROW_LEVELS = 5
COL_LEVELS = 3
HALVES = 2
MESH = pl.DeviceIdType.MESH


def flip(index, mask):
    bit = 1
    while bit <= mask:
        if mask & bit:
            index = index + bit * (1 - 2 * ((index // bit) % 2))
        bit *= 2
    return index


def dot(a, b):
    return jnp.dot(a, b, precision=lax.Precision.HIGHEST, preferred_element_type=jnp.float32)


def schedule(blocks):
    order = sorted(range(blocks), key=lambda k: (-bin(k).count("1"), k))
    when = [(1, 1), (1, 2), (2, 4), (2, 5), (2, 6)]
    steps = []
    for i, (k, h) in enumerate((k, h) for k in order for h in range(HALVES)):
        for level in range(ROW_LEVELS):
            rate, first = when[level]
            steps.append((rate * i + first, -level, k, h))
    return [(k, h, -l, t) for t, l, k, h in sorted(steps, key=lambda s: (s[0], s[1]))]


def kernel(
    n_row, n_col, src, fac, out, xs, f, wb, msend, mrecv, acc, racc, tmp,
    src_sem, fac_sem, s_send, s_recv, m_send, m_recv, a_send, a_recv,
):
    row, col = lax.axis_index("row"), lax.axis_index("col")
    log_row, log_col = n_row.bit_length() - 1, n_col.bit_length() - 1
    levels, blocks, width = f.shape[0], f.shape[1], f.shape[2]
    cw = xs.shape[-1]
    pieces = n_col // blocks
    rows_out = width // pieces
    place = col // pieces
    block_of = [flip(place, k) for k in range(blocks)]

    def row_peer(level):
        return (flip(row, 1 << (level % log_row)), col)

    def col_peer(bit):
        return (row, flip(col, 1 << bit))

    def fold_bit(level):
        return (level - ROW_LEVELS) % log_col

    loads = {}
    for k in range(blocks):
        for h in range(HALVES):
            loads[k, h] = pltpu.make_async_copy(
                src.at[pl.ds(block_of[k] * width, width), pl.ds(h * cw, cw)],
                xs.at[0, k, h, pl.ds(0, width)],
                src_sem.at[k, h],
            )
            loads[k, h].start()
    fac_loads = {}
    for level in [0, levels - 1, levels - 2, 1, 2, levels - 3, 3, 4]:
        for side in range(2):
            fac_loads[level, side] = pltpu.make_async_copy(
                fac.at[level, :, side],
                f.at[level, :, :, pl.ds(side * width, width)],
                fac_sem.at[level, side],
            )
            fac_loads[level, side].start()

    barrier = pltpu.get_barrier_semaphore()
    peers = [row_peer(b) for b in range(min(log_row, ROW_LEVELS))] + [col_peer(b) for b in range(log_col)]
    for peer in peers:
        pl.semaphore_signal(barrier, inc=1, device_id=peer, device_id_type=MESH)
    pl.semaphore_wait(barrier, len(peers))

    copies = []

    def send(source, target, send_sem, recv_sem, peer):
        copy = pltpu.make_async_remote_copy(
            src_ref=source, dst_ref=target, send_sem=send_sem, recv_sem=recv_sem,
            device_id=peer, device_id_type=MESH,
        )
        copy.start()
        copies.append(copy)
        return copy

    steps = schedule(blocks)
    state = {}

    def send_state(level, k, h, source):
        state[level, k, h] = send(
            source, xs.at[level, k, h, pl.ds(width, width)],
            s_send.at[level, k, h], s_recv.at[level, k, h], row_peer(level),
        )

    for k, h, level, _ in steps:
        if level == 0:
            send_state(0, k, h, src.at[pl.ds(block_of[k] * width, width), pl.ds(h * cw, cw)])

    fold = {}
    fold[levels - 1] = send(
        fac.at[levels - 1, :, 1], mrecv.at[COL_LEVELS - 1],
        m_send.at[COL_LEVELS - 1], m_recv.at[COL_LEVELS - 1], col_peer(fold_bit(levels - 1)),
    )

    ready = set()

    def factor(level):
        if level not in ready:
            ready.add(level)
            fac_loads[level, 0].wait()
            fac_loads[level, 1].wait()

    def fold_stage(level):
        factor(level)
        factor(level - 1)
        slot = level - ROW_LEVELS
        fold[level].wait_recv()
        for j in range(blocks):
            own = f[level, j, :, :width] if level == levels - 1 else wb[slot, j]
            both = dot(own + mrecv[slot, j], f[level - 1, j])
            if slot > 0:
                wb[slot - 1, j] = both[:, :width]
                msend[slot - 1, j] = both[:, width:]
            else:
                f[level - 1, j] = both
        if slot > 0:
            fold[level - 1] = send(
                msend.at[slot - 1], mrecv.at[slot - 1],
                m_send.at[slot - 1], m_recv.at[slot - 1], col_peer(fold_bit(level - 1)),
            )

    sums = {}

    def contribute(k, h, value):
        if pieces > 1:
            tmp[...] = value
        for sub in sorted(range(pieces), key=lambda s: (-bin(s).count("1"), s)):
            q = k * pieces + sub
            if pieces > 1:
                start = pl.multiple_of((flip(col, sub) % pieces) * rows_out, rows_out)
                part = tmp[pl.ds(start, rows_out), :]
            else:
                part = value
            low = 0
            while low < log_col and not (q >> low) & 1:
                sums[q | (1 << low), h].wait_recv()
                part = part + racc[q | (1 << low), h]
                low += 1
            if q:
                acc[q, h] = part
                sums[q, h] = send(
                    acc.at[q, h], racc.at[q, h], a_send.at[q, h], a_recv.at[q, h], col_peer(low)
                )
            else:
                out[:, h * cw:(h + 1) * cw] = part

    stages = [(0, levels - 1), (5, levels - 2), (6, levels - 3)]
    for k, h, level, when in steps:
        while stages and when >= stages[0][0] and (len(stages) > 1 or level == ROW_LEVELS - 1):
            fold_stage(stages.pop(0)[1])
        factor(level)
        if level == 0:
            loads[k, h].wait()
        state[level, k, h].wait_recv()
        value = dot(f[level, block_of[k]], xs[level, k, h])
        if level < ROW_LEVELS - 1:
            xs[level + 1, k, h, :width] = value
            send_state(level + 1, k, h, xs.at[level + 1, k, h, pl.ds(0, width)])
        else:
            contribute(k, h, value)
    for copy in copies:
        copy.wait_send()


def shards(sources, level_factors):
    levels, blocks, _, width, _ = level_factors.shape
    columns = sources.shape[1]
    n_row, n_col = lax.axis_size("row"), lax.axis_size("col")
    rows_out = blocks * width // n_col
    cw = columns // HALVES
    dma = pltpu.SemaphoreType.DMA
    return pl.pallas_call(
        functools.partial(kernel, n_row, n_col),
        out_shape=jax.ShapeDtypeStruct((rows_out, columns), jnp.float32),
        in_specs=[pl.BlockSpec(memory_space=pl.ANY)] * 2,
        out_specs=pl.BlockSpec(memory_space=pltpu.VMEM),
        scratch_shapes=[
            pltpu.VMEM((ROW_LEVELS, blocks, HALVES, 2 * width, cw), jnp.float32),
            pltpu.VMEM((levels, blocks, width, 2 * width), jnp.float32),
            pltpu.VMEM((COL_LEVELS - 1, blocks, width, width), jnp.float32),
            pltpu.VMEM((COL_LEVELS - 1, blocks, width, width), jnp.float32),
            pltpu.VMEM((COL_LEVELS, blocks, width, width), jnp.float32),
            pltpu.VMEM((n_col, HALVES, rows_out, cw), jnp.float32),
            pltpu.VMEM((n_col, HALVES, rows_out, cw), jnp.float32),
            pltpu.VMEM((width, cw), jnp.float32),
            dma((blocks, HALVES)),
            dma((levels, 2)),
            dma((ROW_LEVELS, blocks, HALVES)),
            dma((ROW_LEVELS, blocks, HALVES)),
            dma((COL_LEVELS,)),
            dma((COL_LEVELS,)),
            dma((n_col, HALVES)),
            dma((n_col, HALVES)),
        ],
        compiler_params=pltpu.CompilerParams(
            collective_id=0, has_side_effects=True, vmem_limit_bytes=48 * 2**20
        ),
    )(sources, level_factors)


def solution(mesh):
    return jax.shard_map(
        shards,
        mesh=mesh,
        in_specs=(P(("row", "col"), None), P(None, ("row", "col"), None, None, None)),
        out_specs=P(("row", "col"), None),
        check_vma=False,
    )
```

time: 140 us -> 89.6 us (0.64)
  the two profiles are of different devices: /device:TPU:0 before, /device:TPU:20 now
where the time goes in v1:
time: 89.6 us; the launch traced here: 89.5 us
  Pallas kernels  85.6 us (96%)
  local copies, waits for them, and re-layouts  3.89 us (4%)
    pallas_call x1, Pallas kernels, shards(): pl.pallas_call(functools.partial(kernel, n_row, n_col), out_shape=jax.Sha...  85.6 us
    unnamed x5, local copies, waits for them, and re-layouts  3.89 us

profile of v1, /device:TPU:20, one launch (start us, length us, event | category | flops | bytes accessed | tf_op | source)
XLA Modules:
  0.0 89.5 jit_solution(855865578028038339)
XLA Ops:
  0.0 0.0 copy-start
  0.0 2.2 %copy-done = f32[8,4,2,128,128]{4,3,2,1,0:T(8,128)S(1)} copy-done((f32[8,4,2,128,128]{4,3,2,1,0:T(8,128)S(1)}, f32[8,4,2,128,128]{4,3,2,1,0:T(8,128)}, u32[]{:S(2)}) %copy-start) | copy-done | bytes 4194328
  2.2 0.0 copy-start.1
  2.2 1.0 %copy-done.1 = f32[512,256]{1,0:T(8,128)S(1)} copy-done((f32[512,256]{1,0:T(8,128)S(1)}, f32[512,256]{1,0:T(8,128)}, u32[]{:S(2)}) %copy-start.1) | copy-done | bytes 524312
  3.2 85.6 %shard_map.28 = f32[128,256]{1,0:T(8,128)S(1)} custom-call(f32[512,256]{1,0:T(8,128)S(1)} %copy-done.1, f32[8,4,2,128,128]{4,3,2,1,0:T(8,128)S(1)} %copy-done), custom_call_target="tpu_custom_call" | custom-call | tf_op jit(solution)/shard_map/pallas_call | solution.py:194
  88.8 0.7 copy.4
Async XLA Ops:
  0.0 2.2 %copy-start = (f32[8,4,2,128,128]{4,3,2,1,0:T(8,128)S(1)}, f32[8,4,2,128,128]{4,3,2,1,0:T(8,128)}, u32[]{:S(2)}) copy-start(f32[8,4,2,128,128]{4,3,2,1,0:T(8,128)} %fac.1) | copy-start | bytes 12582916
  2.2 1.0 %copy-start.1 = (f32[512,256]{1,0:T(8,128)S(1)}, f32[512,256]{1,0:T(8,128)}, u32[]{:S(2)}) copy-start(f32[512,256]{1,0:T(8,128)} %src.1) | copy-start | bytes 1572868

commit v2 on v1

v2 whole, which is shorter than its diff:
```python
import functools

import jax
import jax.numpy as jnp
from jax import lax
from jax.experimental import pallas as pl
from jax.experimental.pallas import tpu as pltpu
from jax.sharding import PartitionSpec as P

ROW_LEVELS = 5
COL_LEVELS = 3
HALVES = 1
MESH = pl.DeviceIdType.MESH


def flip(index, mask):
    bit = 1
    while bit <= mask:
        if mask & bit:
            index = index + bit * (1 - 2 * ((index // bit) % 2))
        bit *= 2
    return index


def dot(a, b):
    return jnp.dot(a, b, precision=lax.Precision.HIGHEST, preferred_element_type=jnp.float32)


def schedule(blocks):
    order = sorted(range(blocks), key=lambda k: (-bin(k).count("1"), k))
    when = [(1, 1), (1, 2), (1, 3), (1, 4), (1, 5)]
    steps = []
    for i, (k, h) in enumerate((k, h) for k in order for h in range(HALVES)):
        for level in range(ROW_LEVELS):
            rate, first = when[level]
            steps.append((rate * i + first, level, k, h))
    return [(k, h, l, t) for t, l, k, h in sorted(steps, key=lambda s: (s[0], s[1]))]


def kernel(
    n_row, n_col, src, fac, out, xs, f, last, wb, msend, mrecv, acc, racc, tmp,
    src_sem, fac_sem, s_send, s_recv, m_send, m_recv, a_send, a_recv,
):
    row, col = lax.axis_index("row"), lax.axis_index("col")
    log_row, log_col = n_row.bit_length() - 1, n_col.bit_length() - 1
    levels, blocks, width = f.shape[0], f.shape[1], f.shape[3]
    cw = xs.shape[-1]
    pieces = n_col // blocks
    rows_out = width // pieces
    place = col // pieces
    block_of = [flip(place, k) for k in range(blocks)]

    def row_peer(level):
        return (flip(row, 1 << (level % log_row)), col)

    def col_peer(bit):
        return (row, flip(col, 1 << bit))

    def fold_bit(level):
        return (level - ROW_LEVELS) % log_col

    barrier = pltpu.get_barrier_semaphore()
    peers = [row_peer(b) for b in range(min(log_row, ROW_LEVELS))] + [col_peer(b) for b in range(log_col)]
    for peer in peers:
        pl.semaphore_signal(barrier, inc=1, device_id=peer, device_id_type=MESH)
    pl.semaphore_wait(barrier, len(peers))

    copies = []

    def send(source, target, send_sem, recv_sem, peer):
        copy = pltpu.make_async_remote_copy(
            src_ref=source, dst_ref=target, send_sem=send_sem, recv_sem=recv_sem,
            device_id=peer, device_id_type=MESH,
        )
        copy.start()
        copies.append(copy)
        return copy

    steps = schedule(blocks)
    state = {}

    def send_state(level, k, h, source):
        state[level, k, h] = send(
            source, xs.at[level, k, h, pl.ds(width, width)],
            s_send.at[level, k, h], s_recv.at[level, k, h], row_peer(level),
        )

    for k, h, level, _ in steps:
        if level == 0:
            send_state(0, k, h, src.at[pl.ds(block_of[k] * width, width), pl.ds(h * cw, cw)])

    fold = {}
    fold[levels - 1] = send(
        fac.at[levels - 1, :, 1], mrecv.at[COL_LEVELS - 1],
        m_send.at[COL_LEVELS - 1], m_recv.at[COL_LEVELS - 1], col_peer(fold_bit(levels - 1)),
    )

    loads = {}
    for k in range(blocks):
        for h in range(HALVES):
            loads[k, h] = pltpu.make_async_copy(
                src.at[pl.ds(block_of[k] * width, width), pl.ds(h * cw, cw)],
                xs.at[0, k, h, pl.ds(0, width)],
                src_sem.at[k, h],
            )
            loads[k, h].start()
    fac_loads = {}
    for level in [0, levels - 1, levels - 2, 1, 2, levels - 3, 3, 4]:
        fac_loads[level] = pltpu.make_async_copy(fac.at[level], f.at[level], fac_sem.at[level])
        fac_loads[level].start()

    ready = set()

    def factor(level):
        if level not in ready:
            ready.add(level)
            fac_loads[level].wait()

    def pair(level, j):
        if level == ROW_LEVELS - 1:
            return last[j]
        return jnp.concatenate([f[level, j, 0], f[level, j, 1]], axis=1)

    def fold_stage(level):
        factor(level)
        factor(level - 1)
        slot = level - ROW_LEVELS
        fold[level].wait_recv()
        for j in range(blocks):
            own = f[level, j, 0] if level == levels - 1 else wb[slot, j]
            both = dot(
                own + mrecv[slot, j],
                jnp.concatenate([f[level - 1, j, 0], f[level - 1, j, 1]], axis=1),
            )
            if slot > 0:
                wb[slot - 1, j] = both[:, :width]
                msend[slot - 1, j] = both[:, width:]
            else:
                last[j] = both
        if slot > 0:
            fold[level - 1] = send(
                msend.at[slot - 1], mrecv.at[slot - 1],
                m_send.at[slot - 1], m_recv.at[slot - 1], col_peer(fold_bit(level - 1)),
            )

    sums = {}

    def contribute(k, h, value):
        if pieces > 1:
            tmp[...] = value
        for sub in sorted(range(pieces), key=lambda s: (-bin(s).count("1"), s)):
            q = k * pieces + sub
            if pieces > 1:
                start = pl.multiple_of((flip(col, sub) % pieces) * rows_out, rows_out)
                part = tmp[pl.ds(start, rows_out), :]
            else:
                part = value
            low = 0
            while low < log_col and not (q >> low) & 1:
                sums[q | (1 << low), h].wait_recv()
                part = part + racc[q | (1 << low), h]
                low += 1
            if q:
                acc[q, h] = part
                sums[q, h] = send(
                    acc.at[q, h], racc.at[q, h], a_send.at[q, h], a_recv.at[q, h], col_peer(low)
                )
            else:
                out[:, h * cw:(h + 1) * cw] = part

    stages = [(0, levels - 1), (3, levels - 2), (4, levels - 3)]
    for k, h, level, when in steps:
        while stages and when >= stages[0][0]:
            fold_stage(stages.pop(0)[1])
        factor(level)
        if level == 0:
            loads[k, h].wait()
        state[level, k, h].wait_recv()
        value = dot(pair(level, block_of[k]), xs[level, k, h])
        if level < ROW_LEVELS - 1:
            xs[level + 1, k, h, :width] = value
            send_state(level + 1, k, h, xs.at[level + 1, k, h, pl.ds(0, width)])
        else:
            contribute(k, h, value)
    for copy in copies:
        copy.wait_send()


def shards(sources, level_factors):
    levels, blocks, _, width, _ = level_factors.shape
    columns = sources.shape[1]
    n_row, n_col = lax.axis_size("row"), lax.axis_size("col")
    rows_out = blocks * width // n_col
    cw = columns // HALVES
    dma = pltpu.SemaphoreType.DMA
    return pl.pallas_call(
        functools.partial(kernel, n_row, n_col),
        out_shape=jax.ShapeDtypeStruct((rows_out, columns), jnp.float32),
        in_specs=[pl.BlockSpec(memory_space=pltpu.HBM)] * 2,
        out_specs=pl.BlockSpec(memory_space=pltpu.VMEM),
        scratch_shapes=[
            pltpu.VMEM((ROW_LEVELS, blocks, HALVES, 2 * width, cw), jnp.float32),
            pltpu.VMEM((levels, blocks, 2, width, width), jnp.float32),
            pltpu.VMEM((blocks, width, 2 * width), jnp.float32),
            pltpu.VMEM((COL_LEVELS - 1, blocks, width, width), jnp.float32),
            pltpu.VMEM((COL_LEVELS - 1, blocks, width, width), jnp.float32),
            pltpu.VMEM((COL_LEVELS, blocks, width, width), jnp.float32),
            pltpu.VMEM((n_col, HALVES, rows_out, cw), jnp.float32),
            pltpu.VMEM((n_col, HALVES, rows_out, cw), jnp.float32),
            pltpu.VMEM((width, cw), jnp.float32),
            dma((blocks, HALVES)),
            dma((levels,)),
            dma((ROW_LEVELS, blocks, HALVES)),
            dma((ROW_LEVELS, blocks, HALVES)),
            dma((COL_LEVELS,)),
            dma((COL_LEVELS,)),
            dma((n_col, HALVES)),
            dma((n_col, HALVES)),
        ],
        compiler_params=pltpu.CompilerParams(
            collective_id=0, has_side_effects=True, vmem_limit_bytes=48 * 2**20
        ),
    )(sources, level_factors)


def solution(mesh):
    return jax.shard_map(
        shards,
        mesh=mesh,
        in_specs=(P(("row", "col"), None), P(None, ("row", "col"), None, None, None)),
        out_specs=P(("row", "col"), None),
        check_vma=False,
    )
```

time: 89.6 us -> 53.8 us (0.60)
  the two profiles are of different devices: /device:TPU:20 before, /device:TPU:0 now
where the time goes in v2:
time: 53.8 us; the launch traced here: 53.6 us
  Pallas kernels  49.7 us (92%)
  local copies, waits for them, and re-layouts  3.89 us (7%)
    pallas_call x1, Pallas kernels, shards(): pl.pallas_call(functools.partial(kernel, n_row, n_col), out_shape=jax.Sha...  49.7 us
    unnamed x5, local copies, waits for them, and re-layouts  3.89 us

profile of v2, /device:TPU:0, one launch (start us, length us, event | category | flops | bytes accessed | tf_op | source)
XLA Modules:
  0.0 53.6 jit_solution(4602500883125955437)
XLA Ops:
  0.0 0.0 copy-start
  0.0 2.2 %copy-done = f32[8,4,2,128,128]{4,3,2,1,0:T(8,128)S(1)} copy-done((f32[8,4,2,128,128]{4,3,2,1,0:T(8,128)S(1)}, f32[8,4,2,128,128]{4,3,2,1,0:T(8,128)}, u32[]{:S(2)}) %copy-start) | copy-done | bytes 4194328
  2.2 0.0 copy-start.1
  2.2 1.0 %copy-done.1 = f32[512,256]{1,0:T(8,128)S(1)} copy-done((f32[512,256]{1,0:T(8,128)S(1)}, f32[512,256]{1,0:T(8,128)}, u32[]{:S(2)}) %copy-start.1) | copy-done | bytes 524312
  3.2 49.7 %shard_map.28 = f32[128,256]{1,0:T(8,128)S(1)} custom-call(f32[512,256]{1,0:T(8,128)S(1)} %copy-done.1, f32[8,4,2,128,128]{4,3,2,1,0:T(8,128)S(1)} %copy-done), custom_call_target="tpu_custom_call" | custom-call | tf_op jit(solution)/shard_map/pallas_call | solution.py:196
  52.9 0.7 %copy.4 = f32[128,256]{1,0:T(8,128)} copy(f32[128,256]{1,0:T(8,128)S(1)} %shard_map.28) | data formatting | bytes 262144
Async XLA Ops:
  0.0 2.2 %copy-start = (f32[8,4,2,128,128]{4,3,2,1,0:T(8,128)S(1)}, f32[8,4,2,128,128]{4,3,2,1,0:T(8,128)}, u32[]{:S(2)}) copy-start(f32[8,4,2,128,128]{4,3,2,1,0:T(8,128)} %fac.1) | copy-start | bytes 12582916
  2.2 1.0 %copy-start.1 = (f32[512,256]{1,0:T(8,128)S(1)}, f32[512,256]{1,0:T(8,128)}, u32[]{:S(2)}) copy-start(f32[512,256]{1,0:T(8,128)} %src.1) | copy-start | bytes 1572868

commit v3 on v2

--- a/solution.py
+++ b/solution.py
@@ -9,7 +9,10 @@
 
 ROW_LEVELS = 5
 COL_LEVELS = 3
-HALVES = 1
+HALVES = 2
+SPLIT = (True, True)
+BYINDEX = True
+STAGES = (0, 6)
 MESH = pl.DeviceIdType.MESH
 
 
@@ -28,17 +31,21 @@
 
 def schedule(blocks):
     order = sorted(range(blocks), key=lambda k: (-bin(k).count("1"), k))
-    when = [(1, 1), (1, 2), (1, 3), (1, 4), (1, 5)]
-    steps = []
-    for i, (k, h) in enumerate((k, h) for k in order for h in range(HALVES)):
-        for level in range(ROW_LEVELS):
-            rate, first = when[level]
-            steps.append((rate * i + first, level, k, h))
-    return [(k, h, l, t) for t, l, k, h in sorted(steps, key=lambda s: (s[0], s[1]))]
+    parts = []
+    for k in order:
+        if SPLIT[0] and k == order[0] or SPLIT[1] and k == order[-1]:
+            parts += [(k, h, 1) for h in range(HALVES)]
+        else:
+            parts.append((k, 0, HALVES))
+    steps, end = [], 0
+    for i, (k, h, n) in enumerate(parts):
+        end += n / HALVES
+        steps += [((i if BYINDEX else end) + level, level, k, h, n) for level in range(ROW_LEVELS)]
+    return [(k, h, n, level) for _, level, k, h, n in sorted(steps, key=lambda s: s[:2])]
 
 
 def kernel(
-    n_row, n_col, src, fac, out, xs, f, last, wb, msend, mrecv, acc, racc, tmp,
+    n_row, n_col, src, fac, out, first, xs, f, last, wb, msend, mrecv, acc, racc, tmp,
     src_sem, fac_sem, s_send, s_recv, m_send, m_recv, a_send, a_recv,
 ):
     row, col = lax.axis_index("row"), lax.axis_index("col")
@@ -79,15 +86,19 @@
     steps = schedule(blocks)
     state = {}
 
-    def send_state(level, k, h, source):
+    def send_state(level, k, h, n, source):
+        if level == 0:
+            target = first.at[k, pl.ds(width, width), pl.ds(h * cw, n * cw)]
+        else:
+            target = xs.at[level - 1, k, pl.ds(h, n), pl.ds(width, width)]
         state[level, k, h] = send(
-            source, xs.at[level, k, h, pl.ds(width, width)],
-            s_send.at[level, k, h], s_recv.at[level, k, h], row_peer(level),
+            source, target, s_send.at[level, k, h], s_recv.at[level, k, h], row_peer(level)
         )
 
-    for k, h, level, _ in steps:
+    for k, h, n, level in steps:
         if level == 0:
-            send_state(0, k, h, src.at[pl.ds(block_of[k] * width, width), pl.ds(h * cw, cw)])
+            source = src.at[pl.ds(block_of[k] * width, width), pl.ds(h * cw, n * cw)]
+            send_state(0, k, h, n, source)
 
     fold = {}
     fold[levels - 1] = send(
@@ -97,13 +108,10 @@
 
     loads = {}
     for k in range(blocks):
-        for h in range(HALVES):
-            loads[k, h] = pltpu.make_async_copy(
-                src.at[pl.ds(block_of[k] * width, width), pl.ds(h * cw, cw)],
-                xs.at[0, k, h, pl.ds(0, width)],
-                src_sem.at[k, h],
-            )
-            loads[k, h].start()
+        loads[k] = pltpu.make_async_copy(
+            src.at[pl.ds(block_of[k] * width, width)], first.at[k, pl.ds(0, width)], src_sem.at[k]
+        )
+        loads[k].start()
     fac_loads = {}
     for level in [0, levels - 1, levels - 2, 1, 2, levels - 3, 3, 4]:
         fac_loads[level] = pltpu.make_async_copy(fac.at[level], f.at[level], fac_sem.at[level])
@@ -143,45 +151,72 @@
                 m_send.at[slot - 1], m_recv.at[slot - 1], col_peer(fold_bit(level - 1)),
             )
 
+    def side_by_side(ref, h, n):
+        return ref[h] if n == 1 else jnp.concatenate([ref[h + i] for i in range(n)], axis=1)
+
+    def put(ref, h, n, value):
+        for i in range(n):
+            ref[h + i, :value.shape[0]] = value[:, i * cw:(i + 1) * cw]
+
     sums = {}
 
-    def contribute(k, h, value):
+    def landed(q, h, n):
+        for start, halves in list(sums[q]):
+            if start < h + n and h < start + halves:
+                copy = sums[q][start, halves]
+                if copy is not None:
+                    copy.wait_recv()
+                sums[q][start, halves] = None
+        return side_by_side(racc.at[q], h, n)
+
+    def contribute(k, h, n, value):
         if pieces > 1:
-            tmp[...] = value
+            tmp[:, :n * cw] = value
         for sub in sorted(range(pieces), key=lambda s: (-bin(s).count("1"), s)):
             q = k * pieces + sub
             if pieces > 1:
                 start = pl.multiple_of((flip(col, sub) % pieces) * rows_out, rows_out)
-                part = tmp[pl.ds(start, rows_out), :]
+                part = tmp[pl.ds(start, rows_out), :n * cw]
             else:
                 part = value
             low = 0
             while low < log_col and not (q >> low) & 1:
-                sums[q | (1 << low), h].wait_recv()
-                part = part + racc[q | (1 << low), h]
+                part = part + landed(q | (1 << low), h, n)
                 low += 1
             if q:
-                acc[q, h] = part
-                sums[q, h] = send(
-                    acc.at[q, h], racc.at[q, h], a_send.at[q, h], a_recv.at[q, h], col_peer(low)
+                put(acc.at[q], h, n, part)
+                sums.setdefault(q, {})[h, n] = send(
+                    acc.at[q, pl.ds(h, n)], racc.at[q, pl.ds(h, n)],
+                    a_send.at[q, h], a_recv.at[q, h], col_peer(low),
                 )
             else:
-                out[:, h * cw:(h + 1) * cw] = part
-
-    stages = [(0, levels - 1), (3, levels - 2), (4, levels - 3)]
-    for k, h, level, when in steps:
-        while stages and when >= stages[0][0]:
-            fold_stage(stages.pop(0)[1])
+                out[:, h * cw:(h + n) * cw] = part
+
+    stages = {STAGES[i]: levels - 1 - i for i in range(COL_LEVELS - 1)}
+    folded, loaded = False, set()
+    for i, (k, h, n, level) in enumerate(steps):
+        if i in stages:
+            fold_stage(stages[i])
+        if level == ROW_LEVELS - 1 and not folded:
+            fold_stage(ROW_LEVELS)
+            folded = True
         factor(level)
+        if level == 0 and k not in loaded:
+            loads[k].wait()
+            loaded.add(k)
+        state[level, k, h].wait_recv()
         if level == 0:
-            loads[k, h].wait()
-        state[level, k, h].wait_recv()
-        value = dot(pair(level, block_of[k]), xs[level, k, h])
+            block = first[k, :, h * cw:(h + n) * cw]
+        else:
+            block = side_by_side(xs.at[level - 1, k], h, n)
+        value = dot(pair(level, block_of[k]), block)
         if level < ROW_LEVELS - 1:
-            xs[level + 1, k, h, :width] = value
-            send_state(level + 1, k, h, xs.at[level + 1, k, h, pl.ds(0, width)])
-        else:
-            contribute(k, h, value)
+            put(xs.at[level, k], h, n, value)
+            send_state(
+                level + 1, k, h, n, xs.at[level, k, pl.ds(h, n), pl.ds(0, width)]
+            )
+        else:
+            contribute(k, h, n, value)
     for copy in copies:
         copy.wait_send()
 
@@ -199,7 +234,8 @@
         in_specs=[pl.BlockSpec(memory_space=pltpu.HBM)] * 2,
         out_specs=pl.BlockSpec(memory_space=pltpu.VMEM),
         scratch_shapes=[
-            pltpu.VMEM((ROW_LEVELS, blocks, HALVES, 2 * width, cw), jnp.float32),
+            pltpu.VMEM((blocks, 2 * width, columns), jnp.float32),
+            pltpu.VMEM((ROW_LEVELS - 1, blocks, HALVES, 2 * width, cw), jnp.float32),
             pltpu.VMEM((levels, blocks, 2, width, width), jnp.float32),
             pltpu.VMEM((blocks, width, 2 * width), jnp.float32),
             pltpu.VMEM((COL_LEVELS - 1, blocks, width, width), jnp.float32),
@@ -207,8 +243,8 @@
             pltpu.VMEM((COL_LEVELS, blocks, width, width), jnp.float32),
             pltpu.VMEM((n_col, HALVES, rows_out, cw), jnp.float32),
             pltpu.VMEM((n_col, HALVES, rows_out, cw), jnp.float32),
-            pltpu.VMEM((width, cw), jnp.float32),
-            dma((blocks, HALVES)),
+            pltpu.VMEM((width, columns), jnp.float32),
+            dma((blocks,)),
             dma((levels,)),
             dma((ROW_LEVELS, blocks, HALVES)),
             dma((ROW_LEVELS, blocks, HALVES)),

time: 53.8 us -> 52.7 us (0.980)
  Pallas kernels: 49.7 us -> 48.7 us
    pallas_call x1, Pallas kernels: 49.7 us -> 48.7 us  [shards(): pl.pallas_call(functools.partial(kernel, n_row, n_col), out_shape=jax.Sha...]
where the time goes in v3:
time: 52.7 us; the launch traced here: 52.6 us
  Pallas kernels  48.7 us (92%)
  local copies, waits for them, and re-layouts  3.89 us (7%)
    pallas_call x1, Pallas kernels, shards(): pl.pallas_call(functools.partial(kernel, n_row, n_col), out_shape=jax.Sha...  48.7 us
    unnamed x5, local copies, waits for them, and re-layouts  3.89 us

profile of v3, /device:TPU:0, one launch (start us, length us, event | category | flops | bytes accessed | tf_op | source)
XLA Modules:
  0.0 52.6 jit_solution(17424593675047095406)
XLA Ops:
  0.0 0.0 copy-start
  0.0 2.2 %copy-done = f32[8,4,2,128,128]{4,3,2,1,0:T(8,128)S(1)} copy-done((f32[8,4,2,128,128]{4,3,2,1,0:T(8,128)S(1)}, f32[8,4,2,128,128]{4,3,2,1,0:T(8,128)}, u32[]{:S(2)}) %copy-start) | copy-done | bytes 4194328
  2.2 0.0 copy-start.1
  2.2 1.0 %copy-done.1 = f32[512,256]{1,0:T(8,128)S(1)} copy-done((f32[512,256]{1,0:T(8,128)S(1)}, f32[512,256]{1,0:T(8,128)}, u32[]{:S(2)}) %copy-start.1) | copy-done | bytes 524312
  3.2 48.7 %shard_map.28 = f32[128,256]{1,0:T(8,128)S(1)} custom-call(f32[512,256]{1,0:T(8,128)S(1)} %copy-done.1, f32[8,4,2,128,128]{4,3,2,1,0:T(8,128)S(1)} %copy-done), custom_call_target="tpu_custom_call" | custom-call | tf_op jit(solution)/shard_map/pallas_call | solution.py:231
  51.9 0.7 %copy.4 = f32[128,256]{1,0:T(8,128)} copy(f32[128,256]{1,0:T(8,128)S(1)} %shard_map.28) | data formatting | bytes 262144
Async XLA Ops:
  0.0 2.2 %copy-start = (f32[8,4,2,128,128]{4,3,2,1,0:T(8,128)S(1)}, f32[8,4,2,128,128]{4,3,2,1,0:T(8,128)}, u32[]{:S(2)}) copy-start(f32[8,4,2,128,128]{4,3,2,1,0:T(8,128)} %fac.1) | copy-start | bytes 12582916
  2.2 1.0 %copy-start.1 = (f32[512,256]{1,0:T(8,128)S(1)}, f32[512,256]{1,0:T(8,128)}, u32[]{:S(2)}) copy-start(f32[512,256]{1,0:T(8,128)} %src.1) | copy-start | bytes 1572868

commit v4 on v3

--- a/solution.py
+++ b/solution.py
@@ -11,7 +11,6 @@
 COL_LEVELS = 3
 HALVES = 2
 SPLIT = (True, True)
-BYINDEX = True
 STAGES = (0, 6)
 MESH = pl.DeviceIdType.MESH
 
@@ -40,7 +39,7 @@
     steps, end = [], 0
     for i, (k, h, n) in enumerate(parts):
         end += n / HALVES
-        steps += [((i if BYINDEX else end) + level, level, k, h, n) for level in range(ROW_LEVELS)]
+        steps += [(i + 1.5 * level, level, k, h, n) for level in range(ROW_LEVELS)]
     return [(k, h, n, level) for _, level, k, h, n in sorted(steps, key=lambda s: s[:2])]
 
 

time: 52.7 us -> 53.4 us (1.013)
  Pallas kernels: 48.7 us -> 49.3 us
    pallas_call x1, Pallas kernels: 48.7 us -> 49.3 us  [shards(): pl.pallas_call(functools.partial(kernel, n_row, n_col), out_shape=jax.Sha...]
where the time goes in v4:
time: 53.4 us; the launch traced here: 53.2 us
  Pallas kernels  49.3 us (92%)
  local copies, waits for them, and re-layouts  3.89 us (7%)
    pallas_call x1, Pallas kernels, shards(): pl.pallas_call(functools.partial(kernel, n_row, n_col), out_shape=jax.Sha...  49.3 us
    unnamed x5, local copies, waits for them, and re-layouts  3.89 us

profile of v4, /device:TPU:0, one launch (start us, length us, event | category | flops | bytes accessed | tf_op | source)
XLA Modules:
  0.0 53.2 jit_solution(3812186107998867875)
XLA Ops:
  0.0 0.0 copy-start
  0.0 2.2 %copy-done = f32[8,4,2,128,128]{4,3,2,1,0:T(8,128)S(1)} copy-done((f32[8,4,2,128,128]{4,3,2,1,0:T(8,128)S(1)}, f32[8,4,2,128,128]{4,3,2,1,0:T(8,128)}, u32[]{:S(2)}) %copy-start) | copy-done | bytes 4194328
  2.2 0.0 copy-start.1
  2.2 1.0 %copy-done.1 = f32[512,256]{1,0:T(8,128)S(1)} copy-done((f32[512,256]{1,0:T(8,128)S(1)}, f32[512,256]{1,0:T(8,128)}, u32[]{:S(2)}) %copy-start.1) | copy-done | bytes 524312
  3.2 49.3 %shard_map.28 = f32[128,256]{1,0:T(8,128)S(1)} custom-call(f32[512,256]{1,0:T(8,128)S(1)} %copy-done.1, f32[8,4,2,128,128]{4,3,2,1,0:T(8,128)S(1)} %copy-done), custom_call_target="tpu_custom_call" | custom-call | tf_op jit(solution)/shard_map/pallas_call | solution.py:230
  52.5 0.7 %copy.4 = f32[128,256]{1,0:T(8,128)} copy(f32[128,256]{1,0:T(8,128)S(1)} %shard_map.28) | data formatting | bytes 262144
Async XLA Ops:
  0.0 2.2 %copy-start = (f32[8,4,2,128,128]{4,3,2,1,0:T(8,128)S(1)}, f32[8,4,2,128,128]{4,3,2,1,0:T(8,128)}, u32[]{:S(2)}) copy-start(f32[8,4,2,128,128]{4,3,2,1,0:T(8,128)} %fac.1) | copy-start | bytes 12582916
  2.2 1.0 %copy-start.1 = (f32[512,256]{1,0:T(8,128)S(1)}, f32[512,256]{1,0:T(8,128)}, u32[]{:S(2)}) copy-start(f32[512,256]{1,0:T(8,128)} %src.1) | copy-start | bytes 1572868
